TPU v7x, 256 devices: a whole 4x4x8 slice. The times are simulated.
256 devices in a mesh: frame: 32 (over z, x), row: 8 (over y, core).
Axes of the slice: x: 4, y: 4, z: 8, core: 2. Of those that a mesh axis runs over, the one named last changes fastest.
Arguments:
- frames_in: bfloat16 [64, 16, 64, 256], P('frame', 'row'), may hold values from -6 to 6
- w_space: bfloat16 [2304, 256], replicated, may hold values from -0.125 to 0.125
- w_time: bfloat16 [768, 256], replicated, may hold values from -0.21875 to 0.21875
- w_qkv: bfloat16 [256, 768], replicated, may hold values from -11 to 11
- w_out: bfloat16 [256, 256], replicated, may hold values from -0.375 to 0.375
- w_down: bfloat16 [2304, 512], replicated, may hold values from -0.125 to 0.125
- cotangent: bfloat16 [64, 8, 32, 512], P('frame', 'row'), may hold values from -0.046875 to 0.046875
Outputs:
- latent: bfloat16 [64, 8, 32, 512], P('frame', 'row')
- grad_space: float32 [589824], P(('frame', 'row'))
- grad_time: float32 [196608], P(('frame', 'row'))
- grad_qkv: float32 [196608], P(('frame', 'row'))
- grad_proj: float32 [65536], P(('frame', 'row'))
- grad_down: float32 [1179648], P(('frame', 'row'))
All inputs are finite; a program needn't handle non-finite values.
Results may differ from a plain program's by a relative error of at most 0.024.
Values may be sent and summed in bfloat16 or wider, within the bound.
A program may use at most 64 MiB of HBM per device.

v0:
```python
import math

import jax
import jax.numpy as jnp
from jax import lax
from jax.experimental import pallas as pl
from jax.experimental.pallas import tpu as pltpu
from jax.sharding import PartitionSpec as P

epsilon = 1e-06
f32 = jnp.float32
bf16 = jnp.bfloat16
MESH = pl.DeviceIdType.MESH
C = 256
FR, XS, ZS, YS, RS = 32, 4, 8, 4, 8


def nn(a, b):
    return jnp.dot(a, b, preferred_element_type=f32)


def nt(a, b):
    return lax.dot_general(a, b, (((1,), (1,)), ((), ())), preferred_element_type=f32)


def tn(a, b):
    return lax.dot_general(a, b, (((0,), (0,)), ((), ())), preferred_element_type=f32)


def inv_rms(v):
    return lax.rsqrt(jnp.mean(v * v, axis=-1, keepdims=True) + epsilon)


def sigmoid(n):
    return 1.0 / (1.0 + jnp.exp(-n))


def act(v):
    n = v * inv_rms(v)
    return n * sigmoid(n)


def rms_grad(normal, inv, upstream):
    return inv * (upstream - normal * jnp.mean(upstream * normal, axis=-1, keepdims=True))


def act_grad(v, upstream):
    inv = inv_rms(v)
    n = v * inv
    s = sigmoid(n)
    return rms_grad(n, inv, upstream * (s * (1.0 + n * (1.0 - s))))


def iota2(rows, cols):
    return (
        lax.broadcasted_iota(jnp.int32, (rows, cols), 0),
        lax.broadcasted_iota(jnp.int32, (rows, cols), 1),
    )


def one_at(hit):
    return jnp.where(hit, 1.0, 0.0).astype(bf16)


def frame_shift(v, by):
    frame = lax.broadcasted_iota(jnp.int32, v.shape, 0) & 63
    moved = pltpu.roll(v, by % v.shape[0], axis=0)
    keep = frame >= by if by > 0 else frame < 64 + by
    return jnp.where(keep, moved, 0.0)


def pack(m):
    m = m.reshape(FR, 8, C)
    return jnp.concatenate([m[:, :, :128], m[:, :, 128:]], axis=1)


def unpack(t):
    low = t[:, :8, :].reshape(C, 128)
    high = t[:, 8:16, :].reshape(C, 128)
    return jnp.concatenate([low, high], axis=1)


def put(ref, m):
    ref[0] = m[:, :128]
    ref[1] = m[:, 128:]


def every_fourth(ref, start):
    return jnp.concatenate([ref[u, pl.ds(start, 64, stride=4), :] for u in range(2)], axis=1)


def kernel(
    x_hbm, wsp_hbm, wt_hbm, wq_hbm, wo_hbm, wd_hbm, cot_hbm,
    lat_out, g_out,
    xv, wsp, wt, wq, wo, wd, cotv,
    halo_x,
    a1s, a1r, a2s, a2r, a3s, a3r, a4s, a4r,
    tmp, fc, lrow_s, lrow_r, rows8, cc_, halo_c, hp, at_,
    gd, gt, gq_, gp_, gs_,
    cD, rcD, yD, rlD, ryD, zD, rzD,
    cT, rcT, zT, rzT, xT, rxT, finT_s, finT_r,
    c2, rc2, y2, ry2,
    zE, rzE,
    finD_s, finD_r, finE_s, finE_r,
    lsem, sent, hr, ar, cs_r, ys_r, rl_r, zs_r, fs_r, t_r,
):
    fr = lax.axis_index("frame")
    r = lax.axis_index("row")
    z, x = fr >> 2, fr & 3
    y, c = r >> 1, r & 1

    def remote(src, dst, ssem, rsem, dev):
        cp = pltpu.make_async_remote_copy(
            src_ref=src, dst_ref=dst, send_sem=ssem, recv_sem=rsem, device_id=dev, device_id_type=MESH
        )
        cp.start()
        return cp

    def wait_for(ref, sem):
        pltpu.make_async_copy(ref, ref, sem).wait()

    up, down = (r + RS - 1) & 7, (r + 1) & 7
    turned = (y - z) & 3
    last = (turned * 4 + x, (4 + turned) * 4 + x)
    own = (last[0] == fr, last[1] == fr)

    places = (y, x)

    barrier = pltpu.get_barrier_semaphore()

    def tell(dev):
        pl.semaphore_signal(barrier, inc=1, device_id=dev, device_id_type=MESH)

    def far_first(n):
        t = n >> 2
        dz = 4 + (1 - 2 * (t & 1)) * ((t + 1) >> 1)
        return ((z + dz) & 7) * 4 + ((x + n + 1) & 3)

    lax.fori_loop(0, FR - 1, lambda n, carry: (tell((far_first(n), r)), carry)[1], 0)
    for dest in (up, down):
        tell((fr, dest))
    for s in range(2, RS - 1):
        tell((fr, (r + s) & 7))
    for s in range(ZS):
        zs = (z + s) & 7
        for cc in range(2):
            source = (zs * 4 + x, 2 * ((z + zs) & 3) + (c ^ cc))
            if s or cc:
                tell(source)
            else:
                pl.when(jnp.logical_not(own[0] | own[1]))(lambda source=source: tell(source))
    loads = []
    for i, (src, dst) in enumerate(
        ((cot_hbm, cotv), (x_hbm, xv), (wsp_hbm, wsp), (wd_hbm, wd), (wt_hbm, wt), (wq_hbm, wq), (wo_hbm, wo))
    ):
        cp = pltpu.make_async_copy(src, dst, lsem.at[i])
        cp.start()
        loads.append(cp)

    def a2a_start(send, recv, i):
        def step(n, carry):
            k = far_first(n)
            remote(send.at[k], recv.at[fr], sent, ar.at[i], (k, r))
            return carry

        lax.fori_loop(0, FR - 1, step, 0)
        recv[fr] = send[fr]

    def a2a_wait(recv, i):
        wait_for(recv.at[pl.ds(0, FR - 1)], ar.at[i])

    i256, j256 = iota2(C, C)
    k8, f8, h8, w8 = i256 >> 3, (i256 >> 2) & 1, (i256 >> 1) & 1, i256 & 1
    perm_cells = one_at(j256 == h8 * 128 + f8 * 64 + 2 * k8 + w8)
    i512, j512 = iota2(512, C)
    u16 = i512 & 15
    f16, q16 = u16 >> 2, u16 & 3
    jcol = (i512 >> 4) + (u16 >> 3)
    perm_cot = one_at((jcol < 32) & (j512 == q16 * 64 + (f16 & 1) * 32 + jcol))
    loads[0].wait()
    cot_rows = jnp.concatenate(
        [cotv[f, 0, :, 128 * q : 128 * q + 128] for q in range(4) for f in range(2)], axis=0
    )
    a2s[...] = nn(perm_cot, cot_rows).reshape(FR, 16, 128).astype(bf16)

    loads[1].wait()
    xf = jnp.concatenate([xv[0, 0], xv[1, 0], xv[0, 1], xv[1, 1]], axis=0).astype(f32)
    first = act(xf).astype(bf16)
    ip, jp = iota2(C, 128)
    wpos = 2 * (ip >> 3) - 1 + (ip & 3)
    perm_patch = one_at((wpos >= 0) & (wpos < 64) & (jp == ((ip >> 2) & 1) * 64 + wpos))
    a3s[0] = pack(nn(perm_patch, first[:128])).astype(bf16)
    a3s[1] = pack(nn(perm_patch, first[128:])).astype(bf16)
    loads[2].wait()

    def tap(a, b):
        return wsp[(3 * a + b) * C : (3 * a + b + 1) * C, :]

    parts = []
    for b in range(3):
        mid = nn(first, tap(1, b))
        other = jnp.concatenate([nn(first[128:], tap(2, b)), nn(first[:128], tap(0, b))], axis=0)
        parts.append(mid + other)
    pl.semaphore_wait(
        barrier, (FR - 1) + (RS - 1) + 2 * RS - jnp.where(own[0], 1, 0) - jnp.where(own[1], 1, 0)
    )
    halo = [
        remote(x_hbm.at[:, 1], halo_x.at[0], sent, hr.at[0], (fr, down)),
        remote(x_hbm.at[:, 0], halo_x.at[1], sent, hr.at[1], (fr, up)),
    ]
    a2a_start(a2s, a2r, 1)
    halo[0].wait_recv()
    halo[1].wait_recv()
    top = act(jnp.concatenate([halo_x[0, 0], halo_x[0, 1]], axis=0).astype(f32))
    top = jnp.where(r > 0, top, 0.0).astype(bf16)
    bottom = act(jnp.concatenate([halo_x[1, 0], halo_x[1, 1]], axis=0).astype(f32))
    bottom = jnp.where(r < RS - 1, bottom, 0.0).astype(bf16)
    for b in range(3):
        parts[b] = parts[b] + jnp.concatenate([nn(top, tap(0, b)), nn(bottom, tap(2, b))], axis=0)
    col = i256 & 63
    spatial = xf + parts[1]
    spatial = spatial + jnp.where(col > 0, pltpu.roll(parts[0], 1, axis=0), 0.0)
    spatial = spatial + jnp.where(col < 63, pltpu.roll(parts[2], C - 1, axis=0), 0.0)
    a1s[...] = pack(nn(perm_cells, spatial.astype(bf16))).astype(bf16)
    a2a_start(a1s, a1r, 0)
    a2a_start(a3s.at[0], a3r.at[0], 2)

    a2a_wait(a2r, 1)
    got = a2r[...].astype(f32)
    cots = []
    for u in range(2):
        rows8[...] = got[:, 8 * u : 8 * u + 8, :].reshape(C, 128)
        cots.append(
            jnp.concatenate([rows8[pl.ds(q, 64, stride=4), :] for q in range(4)], axis=1).astype(bf16)
        )
        cc_[u] = cots[u]
    cot_cell = cots[0]
    chalo = [remote(cc_, halo_c, sent, hr.at[2], (fr, up))]
    a2a_start(a3s.at[1], a3r.at[1], 4)
    not_top, not_left = r > 0, fr > 0
    not_bottom, not_right = r < RS - 1, fr < FR - 1

    def masked(v, keep):
        return jnp.where(keep, v.astype(f32), 0.0).astype(bf16)

    for i in range(3, 7):
        loads[i].wait()

    a2a_wait(a1r, 0)
    put(tmp, unpack(a1r[...].astype(f32)))
    sp = jnp.concatenate([every_fourth(tmp, cell) for cell in range(4)], axis=0)
    second = act(sp).astype(bf16)
    wtk = [wt[k * C : (k + 1) * C, :] for k in range(3)]
    temporal = sp + nn(second, wtk[2])
    temporal = temporal + frame_shift(nn(second, wtk[1]), 1)
    temporal = temporal + frame_shift(nn(second, wtk[0]), 2)
    temporal = temporal.astype(bf16).astype(f32)
    inv_t = inv_rms(temporal)
    norm_t = temporal * inv_t
    norm_b = norm_t.astype(bf16)

    proj = nn(norm_b, wq[...]).astype(bf16)
    query, key, value = proj[:, :C], proj[:, C : 2 * C], proj[:, 2 * C :]
    scale = 1.0 / math.sqrt(C)
    logits = nt(query, key) * scale
    allowed = ((i256 >> 6) == (j256 >> 6)) & (i256 >= j256)
    logits = jnp.where(allowed, logits, -1e30)
    exponent = jnp.exp(logits - jnp.max(logits, axis=-1, keepdims=True))
    weights = exponent / jnp.sum(exponent, axis=-1, keepdims=True)
    weights_b = weights.astype(bf16)
    mixed = nn(weights_b, value).astype(bf16)
    attended = nn(mixed, wo[...]).astype(bf16).astype(f32)
    residual = (temporal + attended).astype(bf16).astype(f32)
    fourth = act(residual)

    fourth_b = fourth.astype(bf16)
    for cell in range(4):
        fc[cell] = fourth_b[64 * cell : 64 * cell + 64]

    def pack_rows(read, cbuf, rows):
        def step(p, carry):
            s1, pair = p >> 1, p & 1
            at = pl.multiple_of(pair * (2 * rows), 16)
            pairs = ((s1 * 4 + 2 * pair, s1 * 4 + 2 * pair + 1), (16 + 8 * pair + s1, 20 + 8 * pair + s1))
            for h, (one, two) in enumerate(pairs):
                for cc in range(2):
                    both = jnp.concatenate([read(one, cc), read(two, cc)], axis=0)
                    cbuf[cc, h, s1, pl.ds(at, 2 * rows), :] = both.astype(bf16)
            return carry

        lax.fori_loop(0, 8, step, 0)

    def read_d(block, cc):
        at = pl.multiple_of(block * 72, 8)
        return jnp.concatenate(
            [gd[pl.ds(at, 72), cc * 256 + q * 128 : cc * 256 + q * 128 + 128] for q in range(2)], axis=0
        )

    def read_1(block, cc):
        a24, a8 = pl.multiple_of(block * 24, 8), pl.multiple_of(block * 8, 8)
        pieces = [gt[pl.ds(a24, 24), cc * 128 : cc * 128 + 128]]
        pieces += [gq_[pl.ds(a8, 8), cc * 384 + m * 128 : cc * 384 + m * 128 + 128] for m in range(3)]
        pieces += [gp_[pl.ds(a8, 8), cc * 128 : cc * 128 + 128]]
        return jnp.concatenate(pieces, axis=0)

    def read_2(block, cc):
        at = pl.multiple_of(block * 72, 8)
        return gs_[pl.ds(at, 72), cc * 128 : cc * 128 + 128]

    def part(axis, place):
        return (place - z) & 3 if axis == 0 else place

    def core_start(cbuf, rc, i):
        for s in (2, 1, 3, 0):
            for h in range(2):
                j = part(h, (places[h] + s) & 3)
                remote(cbuf.at[1 - c, h, j], rc.at[h, j], sent, cs_r.at[8 * i + 4 * h + s], (fr, r ^ 1))


    def along(axis, j):
        return (fr, 2 * j + c) if axis == 0 else (z * 4 + j, r)

    def pair_sum(cbuf, rc, h, s, p, rows):
        j = part(h, (places[h] + s) & 3)
        here = slice(2 * rows * p, 2 * rows * (p + 1))
        return cbuf[c, h, j, here, :].astype(f32) + rc[h, j, here, :].astype(f32)

    def core_wait(rc, i, s, h):
        j = part(h, (places[h] + s) & 3)
        wait_for(rc.at[h, j], cs_r.at[8 * i + 4 * h + s])

    def send_half(yb, ry, i, h, way, p, rows):
        half = pl.ds(2 * rows * p, 2 * rows)
        place = (places[h] + (1, 3)[way]) & 3
        remote(
            yb.at[h, way, half], ry.at[h, way, half], sent, ys_r.at[2 * i + h], along(h, place)
        )

    def first_start(cbuf, rc, yb, rl, i, rows, hs):
        for h in hs:
            core_wait(rc, i, 2, h)
            for p in range(2):
                half = slice(2 * rows * p, 2 * rows * (p + 1))
                yb[h, 2, half, :] = pair_sum(cbuf, rc, h, 2, p, rows).astype(bf16)
                place = (places[h] + (1, 3)[p]) & 3
                remote(
                    yb.at[h, 2, pl.ds(2 * rows * p, 2 * rows)], rl.at[h, p],
                    sent, rl_r.at[4 * i + 2 * h + p], along(h, place),
                )

    def first_halves(cbuf, rc, yb, ry, i, rows, hs):
        for way in range(2):
            for h in hs:
                p = 1 - way
                core_wait(rc, i, (1, 3)[way], h)
                half = slice(2 * rows * p, 2 * rows * (p + 1))
                yb[h, way, half, :] = pair_sum(cbuf, rc, h, (1, 3)[way], p, rows).astype(bf16)
                send_half(yb, ry, i, h, way, p, rows)

    def direct_start(cbuf, rc, yb, ry, i, rows):
        for s, slot in ((2, 2), (1, 0), (3, 1)):
            for h in range(2):
                core_wait(rc, i, s, h)
                for p in range(2):
                    half = slice(2 * rows * p, 2 * rows * (p + 1))
                    yb[h, slot, half, :] = pair_sum(cbuf, rc, h, s, p, rows).astype(bf16)
                place = (places[h] + s) & 3
                remote(yb.at[h, slot], ry.at[h, slot], sent, ys_r.at[2 * i + h], along(h, place))

    def direct_wait(rc, ry, i, h):
        core_wait(rc, i, 0, h)
        wait_for(ry.at[h], ys_r.at[2 * i + h])

    def first_relay(cbuf, rc, yb, rl, ry, i, rows):
        for h in range(2):
            for way in range(2):
                wait_for(rl.at[h, way], rl_r.at[4 * i + 2 * h + way])
                half = slice(2 * rows * way, 2 * rows * (way + 1))
                total = pair_sum(cbuf, rc, h, (1, 3)[way], way, rows) + rl[h, way].astype(f32)
                yb[h, way, half, :] = total.astype(bf16)
                send_half(yb, ry, i, h, way, way, rows)

    def first_total(cbuf, rc, ry, h, p, rows):
        half = slice(2 * rows * p, 2 * rows * (p + 1))
        total = pair_sum(cbuf, rc, h, 0, p, rows)
        for way in range(ry.shape[1]):
            total = total + ry[h, way, half, :].astype(f32)
        return total

    def first_wait(rc, ry, i, h, rows):
        core_wait(rc, i, 0, h)
        wait_for(ry.at[h], ys_r.at[2 * i + h])

    def second_start(zbuf, rz, i, h):
        for s in (1, 2, 3):
            j = (places[1 - h] + s) & 3
            remote(zbuf.at[h, part(1 - h, j)], rz.at[h, s - 1], sent, zs_r.at[2 * i + h], along(1 - h, j))

    def second_total(zbuf, rz, i, h):
        total = zbuf[h, part(1 - h, places[1 - h])].astype(f32)
        wait_for(rz.at[h], zs_r.at[2 * i + h])
        for s in range(3):
            total = total + rz[h, s].astype(f32)
        return total

    mine = 2 * z + c

    def last_start(fin_s, fin_r, i, h):
        for s in range(RS):
            dest = (r + s) & 7

            def send(dest=dest):
                remote(fin_s.at[h, dest], fin_r.at[mine], sent, fs_r.at[i], (last[h], dest))

            if s:
                send()
            else:
                pl.when(jnp.logical_not(own[h]))(send)

                @pl.when(own[h])
                def _():
                    fin_r[mine] = fin_s[h, r]

    def last_wait(fin_r, i):
        @pl.when(own[0] | own[1])
        def _():
            wait_for(fin_r.at[pl.ds(0, 15)], fs_r.at[i])

        @pl.when(jnp.logical_not(own[0] | own[1]))
        def _():
            wait_for(fin_r, fs_r.at[i])

    def last_total(fin_r, cc):
        total = fin_r[cc].astype(f32)
        for zs in range(1, ZS):
            total = total + fin_r[2 * zs + cc].astype(f32)
        return total

    def t_pack():
        def step(p, carry):
            zd, pair = p >> 1, p & 1
            at = pl.multiple_of(pair * 112, 16)
            block = zd * 4 + 2 * pair
            for cc in range(2):
                both = jnp.concatenate([read_1(block, cc), read_1(block + 1, cc)], axis=0)
                cT[cc, zd, pl.ds(at, 112), :] = both.astype(bf16)
            return carry

        lax.fori_loop(0, 16, step, 0)
        for s in (4, 3, 5, 2, 6, 1, 7, 0):
            zd = (z + s) & 7
            remote(cT.at[1 - c, zd], rcT.at[zd], sent, t_r.at[s], (fr, r ^ 1))

    def t_start():
        for s in (4, 3, 5, 2, 6, 1, 7):
            zd = (z + s) & 7
            wait_for(rcT.at[zd], t_r.at[s])
            zT[zd] = (cT[c, zd].astype(f32) + rcT[zd].astype(f32)).astype(bf16)
            remote(zT.at[zd], rzT.at[s - 1], sent, t_r.at[8], (zd * 4 + x, r))

    def t_second():
        wait_for(rcT.at[z], t_r.at[0])
        total = cT[c, z].astype(f32) + rcT[z].astype(f32)
        wait_for(rzT, t_r.at[8])
        for s in range(1, ZS):
            total = total + rzT[s - 1].astype(f32)
        gap = jnp.zeros((8, 128), f32)
        for j in range(XS):
            xT[j] = jnp.concatenate([total[56 * j : 56 * j + 56], gap], axis=0).astype(bf16)
        for s in (1, 2, 3):
            j = (x + s) & 3
            remote(xT.at[j], rxT.at[s - 1], sent, t_r.at[9], (z * 4 + j, r))

    def t_last():
        total = xT[x].astype(f32)
        wait_for(rxT, t_r.at[9])
        for s in (1, 2, 3):
            total = total + rxT[s - 1].astype(f32)
        total = jnp.concatenate([total.astype(bf16), jnp.zeros((64, 128), bf16)], axis=0)
        it, jt = iota2(128, 128)
        dt, ut = it >> 4, it & 15
        source = jnp.where(ut < 3, dt * 3 + ut, jnp.where(ut < 6, 24 + (ut - 3) * 8 + dt, 48 + dt))
        perm_t = one_at((ut < 7) & (jt == source))
        finT_s[...] = nn(perm_t, total).reshape(RS, 16, 128).astype(bf16)
        for s in range(1, RS):
            dest = (r + s) & 7
            remote(finT_s.at[dest], finT_r.at[r], sent, t_r.at[10], (fr, dest))
        finT_r[r] = finT_s[r]

    def t_finish():
        wait_for(finT_r.at[pl.ds(0, 7)], t_r.at[10])
        for cc in range(2):
            total = finT_r[cc].astype(f32)
            for ys in range(1, YS):
                total = total + finT_r[2 * ys + cc].astype(f32)
            g_out[pl.ds(24 + cc, 3, stride=2), :] = total[0:3]
            g_out[32 + 3 * cc : 35 + 3 * cc, :] = total[3:6]
            g_out[40 + cc : 41 + cc, :] = total[6:7]

    for h in chalo:
        h.wait_recv()
    shifted = (
        tuple(cots),
        (masked(halo_c[0], not_bottom), masked(halo_c[1], not_bottom)),
    )
    cots_of = (
        (3, 1, 1), (2, 1, 0), (3, 1, 0),
        (1, 0, 1), (0, 0, 0), (1, 0, 0),
        (3, 0, 1), (2, 0, 0), (3, 0, 0),
    )
    for t, (cell, rs, cs) in enumerate(cots_of):
        gd[t * C : (t + 1) * C, :] = tn(fc[cell], shifted[rs][cs])

    pack_rows(read_d, cD, 144)
    core_start(cD, rcD, 0)

    taps_of = {0: ((1, 0),), 1: ((0, 1), (2, 0))}
    blocks = []
    for rp in range(2):
        for cp_ in range(2):
            total = None
            for a, rs in taps_of[rp]:
                for b, cs in taps_of[cp_]:
                    term = nt(shifted[rs][cs], wd[(3 * a + b) * C : (3 * a + b + 1) * C, :])
                    total = term if total is None else total + term
            blocks.append(total)
    grad_fourth = jnp.concatenate(blocks, axis=0)

    grad_res = act_grad(residual, grad_fourth)
    grad_res_b = grad_res.astype(bf16)
    gp_[...] = tn(mixed, grad_res_b)
    grad_mixed = nt(grad_res_b, wo[...]).astype(bf16)

    perm_frames = one_at(j256 == (i256 & 3) * 64 + 2 * k8 + f8)
    a4s[...] = pack(nn(perm_frames, fourth_b)).astype(bf16)
    a2a_start(a4s, a4r, 3)

    a2a_wait(a3r.at[0], 2)
    a2a_wait(a3r.at[1], 4)
    phalo = [
        remote(a3r.at[1], hp.at[0], sent, hr.at[4], (fr, down)),
        remote(a3r.at[0], hp.at[1], sent, hr.at[5], (fr, up)),
    ]
    first_start(cD, rcD, yD, rlD, 0, 144, (1,))

    grad_w = nt(grad_mixed, value)
    grad_s = (
        weights * (grad_w - jnp.sum(grad_w * weights, axis=-1, keepdims=True)) * scale
    ).astype(bf16)
    grad_v = tn(weights_b, grad_mixed).astype(bf16)
    grad_q = nn(grad_s, key).astype(bf16)
    grad_k = tn(grad_s, query).astype(bf16)
    grad_proj = jnp.concatenate([grad_q, grad_k, grad_v], axis=1)
    grad_n = nt(grad_proj, wq[...]).astype(bf16).astype(f32)
    gq_[...] = tn(norm_b, grad_proj)
    grad_t = grad_res + rms_grad(norm_t, inv_t, grad_n)
    grad_tb = grad_t.astype(bf16)
    grad_tb32 = grad_tb.astype(f32)


    gt[0:C, :] = tn(second, frame_shift(grad_tb32, -2).astype(bf16))
    gt[C : 2 * C, :] = tn(second, frame_shift(grad_tb32, -1).astype(bf16))
    gt[2 * C :, :] = tn(second, grad_tb)
    t_pack()

    grad_second = nt(grad_tb, wtk[2])
    grad_second = grad_second + frame_shift(nt(grad_tb, wtk[1]), -1)
    grad_second = grad_second + frame_shift(nt(grad_tb, wtk[0]), -2)
    grad_sb = (grad_t + act_grad(sp, grad_second)).astype(bf16)

    first_start(cD, rcD, yD, rlD, 0, 144, (0,))
    first_halves(cD, rcD, yD, ryD, 0, 144, (1,))
    t_start()
    first_halves(cD, rcD, yD, ryD, 0, 144, (0,))

    for h in phalo:
        h.wait_recv()
    rows_in = (masked(hp[0], not_top), a3r[0], a3r[1], masked(hp[1], not_bottom))
    for hh in range(4):
        put(tmp, unpack(rows_in[hh].astype(f32)))
        cells = [every_fourth(tmp, ww) for ww in range(4)]
        for b in range(3):
            pair = jnp.concatenate([cells[b], cells[b + 1]], axis=0)
            at_[b, :, 128 * hh : 128 * hh + 128] = pair.T.astype(bf16)
    for a in range(3):
        for b in range(3):
            gs_[(3 * a + b) * C : (3 * a + b + 1) * C, :] = nn(at_[b, :, 128 * a : 128 * a + 256], grad_sb)
    pack_rows(read_2, c2, 72)
    core_start(c2, rc2, 1)

    first_relay(cD, rcD, yD, rlD, ryD, 0, 144)
    direct_start(c2, rc2, y2, ry2, 1, 72)

    for h in range(2):
        first_wait(rcD, ryD, 0, h, 144)
        for p in range(2):
            total = first_total(cD, rcD, ryD, h, p, 144).astype(bf16)
            zD[h, 2 * p] = total[:144]
            zD[h, 2 * p + 1] = total[144:]
        second_start(zD, rzD, 0, h)
    a2a_wait(a4r, 3)
    put(tmp, unpack(a4r[...].astype(f32)))
    first_col = lax.broadcasted_iota(jnp.int32, (32, C), 0) == 0
    cells_of = [
        [
            [
                jnp.concatenate(
                    [tmp[u, pl.ds(4 * f + 2 * hh + wp, 32, stride=8), :] for u in range(2)], axis=1
                ).astype(bf16)
                for wp in range(2)
            ]
            for hh in range(2)
        ]
        for f in range(2)
    ]
    for f in range(2):
        for wp in range(2):
            lrow_s[f, wp] = cells_of[f][1][wp]
    lhalo = remote(lrow_s, lrow_r, sent, hr.at[3], (fr, down))
    gap = jnp.zeros((8, 128), f32)
    for h in range(2):
        direct_wait(rc2, ry2, 1, h)
        for p in range(2):
            total = first_total(c2, rc2, ry2, h, p, 72)
            zE[h, 2 * p] = jnp.concatenate([total[:72], gap], axis=0).astype(bf16)
            zE[h, 2 * p + 1] = jnp.concatenate([total[72:], gap], axis=0).astype(bf16)
        second_start(zE, rzE, 1, h)

    it, jt = iota2(128, C)
    dt, ut = it >> 4, it & 15
    perm_d = one_at(jt == jnp.where(ut < 9, 0, 63) + dt * 9 + ut)
    perm_e = one_at((ut < 9) & (jt == dt * 9 + ut))
    perm_r = one_at((ut >= 9) & (ut < 11) & (jt == 70 + dt * 9 + ut))

    def widened(total, rows):
        return jnp.concatenate([total.astype(bf16), jnp.zeros((C - rows, 128), bf16)], axis=0)

    rest = []
    for h in range(2):
        total = widened(second_total(zD, rzD, 0, h), 144)
        finD_s[h] = nn(perm_d, total).reshape(RS, 16, 128).astype(bf16)
        last_start(finD_s, finD_r, 0, h)
        rest.append(nn(perm_r, total))
    t_second()
    for h in range(2):
        total = widened(second_total(zE, rzE, 1, h), 80)
        finE_s[h] = (nn(perm_e, total) + rest[h]).reshape(RS, 16, 128).astype(bf16)
        last_start(finE_s, finE_r, 1, h)

    lhalo.wait_recv()
    taps_in = []
    for a in range(3):
        here = [
            [masked(lrow_r[f, wp], not_top) if a == 0 else cells_of[f][a - 1][wp] for wp in range(2)]
            for f in range(2)
        ]
        for b in range(3):
            picked = [here[f][1 if b != 1 else 0].astype(f32) for f in range(2)]
            if b == 0:
                picked = [jnp.where(first_col, 0.0, pltpu.roll(v, 1, axis=0)) for v in picked]
            taps_in.append(jnp.concatenate(picked, axis=0).astype(bf16))
    latent = None
    for t in range(9):
        term = nn(taps_in[t], wd[t * C : (t + 1) * C, :])
        latent = term if latent is None else latent + term
    for f in range(2):
        lat_out[f, 0] = latent[32 * f : 32 * f + 32].astype(bf16)
    t_last()

    last_wait(finD_r, 0)
    for cc in range(2):
        total = last_total(finD_r, cc)
        g_out[pl.ds(48 + 2 * cc, 9, stride=4), :] = total[0:9]
        g_out[pl.ds(49 + 2 * cc, 7, stride=4), :] = total[9:16]
    last_wait(finE_r, 1)
    for cc in range(2):
        total = last_total(finE_r, cc)
        g_out[pl.ds(cc, 9, stride=2), :] = total[0:9]
        g_out[pl.ds(77 + 2 * cc, 2, stride=4), :] = total[9:11]
    t_finish()
    for h in halo + chalo + phalo + [lhalo]:
        h.wait_send()
    for send in (a1s, a2s, a3s.at[0], a3s.at[1], a4s):
        wait_for(send.at[pl.ds(0, FR - 1)], sent)
    for ref in (rcD, rlD, ryD, rzD, rc2, ry2, rzE, rcT, rzT, rxT, finT_s.at[pl.ds(0, 7)]):
        wait_for(ref, sent)
    for fin_s in (finD_s, finE_s):
        for h in range(2):
            wait_for(fin_s.at[h, pl.ds(0, 7)], sent)
            pl.when(jnp.logical_not(own[h]))(lambda fin_s=fin_s, h=h: wait_for(fin_s.at[h, 0], sent))


starts = (0, 24, 32, 40, 48)


def outputs(lat, g, lat_out, *outs):
    lat_out[...] = lat[...]
    for at, out in zip(starts, outs):
        out[...] = g[at : at + out.shape[0], :]


def per_device(frames_in, w_space, w_time, w_qkv, w_out, w_down, cotangent):
    def vb(*shape):
        return pltpu.VMEM(shape, bf16)

    def vf(*shape):
        return pltpu.VMEM(shape, f32)

    dma = pltpu.SemaphoreType.DMA
    scratch = [
        vb(2, 2, 64, C), vb(9 * C, C), vb(3 * C, C), vb(C, 3 * C), vb(C, C), vb(9 * C, 512), vb(2, 1, 32, 512),
        vb(2, 2, 64, C),
        vb(FR, 16, 128), vb(FR, 16, 128), vb(FR, 16, 128), vb(FR, 16, 128),
        vb(2, FR, 16, 128), vb(2, FR, 16, 128), vb(FR, 16, 128), vb(FR, 16, 128),
        vf(2, C, 128), vb(4, 64, C), vb(2, 2, 32, C), vb(2, 2, 32, C), vf(C, 128),
        vb(2, 64, 512), vb(2, 64, 512), vb(2, FR, 16, 128), vb(3, C, 512),
        vf(9 * C, 512), vf(3 * C, C), vf(C, 3 * C), vf(C, C), vf(9 * C, C),
    ]
    for rows in (144, 72):
        n = 4 * rows
        scratch += [vb(2, 2, 4, n, 128), vb(2, 4, n, 128), vb(2, 3, n, 128)]
        if rows == 144:
            scratch += [vb(2, 2, n // 2, 128), vb(2, 2, n, 128), vb(2, 4, 144, 128), vb(2, 3, 144, 128)]
            scratch += [vb(2, 8, 224, 128), vb(8, 224, 128), vb(8, 224, 128), vb(7, 224, 128)]
            scratch += [vb(4, 64, 128), vb(3, 64, 128), vb(8, 16, 128), vb(8, 16, 128)]
        else:
            scratch += [vb(2, 3, n, 128)]
    scratch += [vb(2, 4, 80, 128), vb(2, 3, 80, 128)]
    scratch += [vb(2, 8, 16, 128), vb(16, 16, 128), vb(2, 8, 16, 128), vb(16, 16, 128)]
    scratch += [
        dma((7,)), dma, dma((6,)), dma((5,)), dma((16,)), dma((4,)), dma((4,)), dma((4,)), dma((2,)), dma((11,)),
    ]
    anywhere = pl.BlockSpec(memory_space=pl.ANY)
    inside = pl.BlockSpec(memory_space=pltpu.VMEM)
    latent, grads = pl.pallas_call(
        kernel,
        out_shape=(vb(2, 1, 32, 512), vf(88, 128)),
        in_specs=[anywhere] * 7,
        out_specs=(inside, inside),
        scratch_shapes=scratch,
        compiler_params=pltpu.CompilerParams(has_side_effects=True, collective_id=0, vmem_limit_bytes=56 * 1024 * 1024),
        cost_estimate=pl.CostEstimate(flops=3 * 10**9, bytes_accessed=10**7, transcendentals=10**6),
    )(frames_in, w_space, w_time, w_qkv, w_out, w_down, cotangent)
    latent = pltpu.with_memory_space_constraint(latent, pltpu.VMEM)
    grads = pltpu.with_memory_space_constraint(grads, pltpu.VMEM)
    rows = (18, 6, 6, 2, 36)
    shapes = [latent.shape] + [(n, 128) for n in rows]
    results = pl.pallas_call(
        outputs,
        out_shape=[jax.ShapeDtypeStruct(v, f32 if i else bf16) for i, v in enumerate(shapes)],
        in_specs=[inside] * 2,
        out_specs=[inside] * 6,
    )(latent, grads)
    return (results[0],) + tuple(v.reshape(-1) for v in results[1:])


def solution(mesh):
    held = P("frame", "row", None, None)
    flat = P(("frame", "row"))
    return jax.shard_map(
        per_device,
        mesh=mesh,
        in_specs=(held, P(), P(), P(), P(), P(), held),
        out_specs=(held, flat, flat, flat, flat, flat),
        check_vma=False,
    )
```

profile of v0, /device:TPU:1, one launch (start us, length us, event | category | flops | bytes accessed | tf_op | source)
XLA Modules:
  0.0 53.2 jit_solution(1411340204282055761)
XLA Ops:
  0.6 51.9 %shard_map.118 = (bf16[2,1,32,512]{3,2,1,0:T(8,128)(2,1)S(1)}, f32[88,128]{1,0:T(8,128)S(1)}) custom-call(bf16[2,2,64,256]{3,2,1,0:T(8,128)(2,1)} %x_hbm.1, bf16[2304,256]{1,0:T(8,128)(2,1)} %wsp_hbm.1, bf16[768,256]{1,0:T(8,128)(2,1)} %wt_hbm.1, bf16[256,768]{1,0:T(8,128)(2,1)} %wq_hbm.1, bf16[256,256]{1,0:T(8,128)(2,1)} %wo_hbm.1, ...), custom_call_target="tpu_custom_call" | custom-call | flops 3000000000 | bytes 10000000 | tf_op jit(solution)/shard_map/pallas_call | solution.py:735
  52.6 0.7 %shard_map.119 = (bf16[2,1,32,512]{3,2,1,0:T(8,128)(2,1)}, f32[18,128]{1,0:T(8,128)}, f32[6,128]{1,0:T(8,128)}, f32[6,128]{1,0:T(8,128)}, f32[2,128]{1,0:T(2,128)}, /*index=5*/f32[36,128]{1,0:T(8,128)}) custom-call(bf16[2,1,32,512]{3,2,1,0:T(8,128)(2,1)S(1)} %get-tuple-element.14.lat, f32[88,128]{1,0:T(8,128)S(1)} %get-tuple-element.15.g), custom_call_target="tpu_custom_call" | custom-call | tf_op jit(solution)/shard_map/pallas_call | solution.py:748
where the time goes:
time: 53.3 us; the launch traced here: 53.2 us
  Pallas kernels  52.6 us (99%)
  between operations  0.64 us (1%)
    pallas_call x1, Pallas kernels, per_device(): pl.pallas_call(kernel, out_shape=(vb(2, 1, 32, 512), vf(88, 128)), in_spe...  51.9 us

commit v1 on v0

--- a/solution.py
+++ b/solution.py
@@ -95,10 +95,10 @@
     xv, wsp, wt, wq, wo, wd, cotv,
     halo_x,
     a1s, a1r, a2s, a2r, a3s, a3r, a4s, a4r,
-    tmp, fc, lrow_s, lrow_r, rows8, cc_, halo_c, hp, at_,
+    tmp, lrow_s, lrow_r, rows8, cc_, halo_c, hp, at_,
     gd, gt, gq_, gp_, gs_,
     cD, rcD, yD, rlD, ryD, zD, rzD,
-    cT, rcT, zT, rzT, xT, rxT, finT_s, finT_r,
+    cT, rcT, zT, rzT, finT_s, finT_r,
     c2, rc2, y2, ry2,
     zE, rzE,
     finD_s, finD_r, finE_s, finE_r,
@@ -149,6 +149,10 @@
                 tell(source)
             else:
                 pl.when(jnp.logical_not(own[0] | own[1]))(lambda source=source: tell(source))
+    for s in range(1, XS):
+        for dr in range(1, RS):
+            tell((z * 4 + ((x + s) & 3), (r + dr) & 7))
+
     loads = []
     for i, (src, dst) in enumerate(
         ((cot_hbm, cotv), (x_hbm, xv), (wsp_hbm, wsp), (wd_hbm, wd), (wt_hbm, wt), (wq_hbm, wq), (wo_hbm, wo))
@@ -202,7 +206,7 @@
         other = jnp.concatenate([nn(first[128:], tap(2, b)), nn(first[:128], tap(0, b))], axis=0)
         parts.append(mid + other)
     pl.semaphore_wait(
-        barrier, (FR - 1) + (RS - 1) + 2 * RS - jnp.where(own[0], 1, 0) - jnp.where(own[1], 1, 0)
+        barrier, (FR - 1) + (RS - 1) + 21 + 2 * RS - jnp.where(own[0], 1, 0) - jnp.where(own[1], 1, 0)
     )
     halo = [
         remote(x_hbm.at[:, 1], halo_x.at[0], sent, hr.at[0], (fr, down)),
@@ -246,6 +250,13 @@
     for i in range(3, 7):
         loads[i].wait()
 
+    def down_tap(a, b, v):
+        return nt(v, wd[(3 * a + b) * C : (3 * a + b + 1) * C, :])
+
+    grad_own = [
+        [down_tap(a, 1, cots[0]), down_tap(a, 0, cots[1]) + down_tap(a, 2, cots[0])] for a in (1, 2)
+    ]
+
     a2a_wait(a1r, 0)
     put(tmp, unpack(a1r[...].astype(f32)))
     sp = jnp.concatenate([every_fourth(tmp, cell) for cell in range(4)], axis=0)
@@ -274,8 +285,6 @@
     fourth = act(residual)
 
     fourth_b = fourth.astype(bf16)
-    for cell in range(4):
-        fc[cell] = fourth_b[64 * cell : 64 * cell + 64]
 
     def pack_rows(read, cbuf, rows):
         def step(p, carry):
@@ -458,41 +467,35 @@
             zT[zd] = (cT[c, zd].astype(f32) + rcT[zd].astype(f32)).astype(bf16)
             remote(zT.at[zd], rzT.at[s - 1], sent, t_r.at[8], (zd * 4 + x, r))
 
-    def t_second():
+    plane = x * RS + r
+
+    def t_last():
         wait_for(rcT.at[z], t_r.at[0])
         total = cT[c, z].astype(f32) + rcT[z].astype(f32)
         wait_for(rzT, t_r.at[8])
         for s in range(1, ZS):
             total = total + rzT[s - 1].astype(f32)
-        gap = jnp.zeros((8, 128), f32)
-        for j in range(XS):
-            xT[j] = jnp.concatenate([total[56 * j : 56 * j + 56], gap], axis=0).astype(bf16)
-        for s in (1, 2, 3):
-            j = (x + s) & 3
-            remote(xT.at[j], rxT.at[s - 1], sent, t_r.at[9], (z * 4 + j, r))
-
-    def t_last():
-        total = xT[x].astype(f32)
-        wait_for(rxT, t_r.at[9])
-        for s in (1, 2, 3):
-            total = total + rxT[s - 1].astype(f32)
-        total = jnp.concatenate([total.astype(bf16), jnp.zeros((64, 128), bf16)], axis=0)
-        it, jt = iota2(128, 128)
-        dt, ut = it >> 4, it & 15
+        total = jnp.concatenate([total.astype(bf16), jnp.zeros((32, 128), bf16)], axis=0)
+        it, jt = iota2(512, C)
+        xt, dt, ut = it >> 7, (it >> 4) & 7, it & 15
         source = jnp.where(ut < 3, dt * 3 + ut, jnp.where(ut < 6, 24 + (ut - 3) * 8 + dt, 48 + dt))
-        perm_t = one_at((ut < 7) & (jt == source))
-        finT_s[...] = nn(perm_t, total).reshape(RS, 16, 128).astype(bf16)
-        for s in range(1, RS):
-            dest = (r + s) & 7
-            remote(finT_s.at[dest], finT_r.at[r], sent, t_r.at[10], (fr, dest))
-        finT_r[r] = finT_s[r]
+        perm_t = one_at((ut < 7) & (jt == xt * 56 + source))
+        finT_s[...] = nn(perm_t, total).reshape(32, 16, 128).astype(bf16)
+
+        def step(n, carry):
+            dest = (plane + n) & 31
+            remote(finT_s.at[dest], finT_r.at[plane], sent, t_r.at[9], (z * 4 + (dest >> 3), dest & 7))
+            return carry
+
+        lax.fori_loop(1, 32, step, 0)
+        finT_r[plane] = finT_s[plane]
 
     def t_finish():
-        wait_for(finT_r.at[pl.ds(0, 7)], t_r.at[10])
+        wait_for(finT_r.at[pl.ds(0, 31)], t_r.at[9])
         for cc in range(2):
             total = finT_r[cc].astype(f32)
-            for ys in range(1, YS):
-                total = total + finT_r[2 * ys + cc].astype(f32)
+            for chip in range(1, XS * YS):
+                total = total + finT_r[2 * chip + cc].astype(f32)
             g_out[pl.ds(24 + cc, 3, stride=2), :] = total[0:3]
             g_out[32 + 3 * cc : 35 + 3 * cc, :] = total[3:6]
             g_out[40 + cc : 41 + cc, :] = total[6:7]
@@ -508,40 +511,39 @@
         (1, 0, 1), (0, 0, 0), (1, 0, 0),
         (3, 0, 1), (2, 0, 0), (3, 0, 0),
     )
+    turned_cells = [fourth[64 * cell : 64 * cell + 64].T.astype(bf16) for cell in range(4)]
     for t, (cell, rs, cs) in enumerate(cots_of):
-        gd[t * C : (t + 1) * C, :] = tn(fc[cell], shifted[rs][cs])
+        gd[t * C : (t + 1) * C, :] = nn(turned_cells[cell], shifted[rs][cs])
 
     pack_rows(read_d, cD, 144)
     core_start(cD, rcD, 0)
 
-    taps_of = {0: ((1, 0),), 1: ((0, 1), (2, 0))}
-    blocks = []
-    for rp in range(2):
-        for cp_ in range(2):
-            total = None
-            for a, rs in taps_of[rp]:
-                for b, cs in taps_of[cp_]:
-                    term = nt(shifted[rs][cs], wd[(3 * a + b) * C : (3 * a + b + 1) * C, :])
-                    total = term if total is None else total + term
-            blocks.append(total)
-    grad_fourth = jnp.concatenate(blocks, axis=0)
+    below = shifted[1]
+    grad_fourth = jnp.concatenate(
+        grad_own[0]
+        + [
+            grad_own[1][0] + down_tap(0, 1, below[0]),
+            grad_own[1][1] + down_tap(0, 0, below[1]) + down_tap(0, 2, below[0]),
+        ],
+        axis=0,
+    )
+
+    a2a_wait(a3r.at[0], 2)
+    phalo = [remote(a3r.at[0], hp.at[1], sent, hr.at[5], (fr, up))]
 
     grad_res = act_grad(residual, grad_fourth)
     grad_res_b = grad_res.astype(bf16)
     gp_[...] = tn(mixed, grad_res_b)
     grad_mixed = nt(grad_res_b, wo[...]).astype(bf16)
 
+    first_start(cD, rcD, yD, rlD, 0, 144, (1,))
+
     perm_frames = one_at(j256 == (i256 & 3) * 64 + 2 * k8 + f8)
     a4s[...] = pack(nn(perm_frames, fourth_b)).astype(bf16)
     a2a_start(a4s, a4r, 3)
 
-    a2a_wait(a3r.at[0], 2)
     a2a_wait(a3r.at[1], 4)
-    phalo = [
-        remote(a3r.at[1], hp.at[0], sent, hr.at[4], (fr, down)),
-        remote(a3r.at[0], hp.at[1], sent, hr.at[5], (fr, up)),
-    ]
-    first_start(cD, rcD, yD, rlD, 0, 144, (1,))
+    phalo.append(remote(a3r.at[1], hp.at[0], sent, hr.at[4], (fr, down)))
 
     grad_w = nt(grad_mixed, value)
     grad_s = (
@@ -558,9 +560,10 @@
     grad_tb32 = grad_tb.astype(f32)
 
 
-    gt[0:C, :] = tn(second, frame_shift(grad_tb32, -2).astype(bf16))
-    gt[C : 2 * C, :] = tn(second, frame_shift(grad_tb32, -1).astype(bf16))
-    gt[2 * C :, :] = tn(second, grad_tb)
+    turned_second = second.astype(f32).T.astype(bf16)
+    gt[0:C, :] = nn(turned_second, frame_shift(grad_tb32, -2).astype(bf16))
+    gt[C : 2 * C, :] = nn(turned_second, frame_shift(grad_tb32, -1).astype(bf16))
+    gt[2 * C :, :] = nn(turned_second, grad_tb)
     t_pack()
 
     grad_second = nt(grad_tb, wtk[2])
@@ -635,17 +638,15 @@
     def widened(total, rows):
         return jnp.concatenate([total.astype(bf16), jnp.zeros((C - rows, 128), bf16)], axis=0)
 
-    rest = []
     for h in range(2):
-        total = widened(second_total(zD, rzD, 0, h), 144)
-        finD_s[h] = nn(perm_d, total).reshape(RS, 16, 128).astype(bf16)
+        total_d = widened(second_total(zD, rzD, 0, h), 144)
+        finD_s[h] = nn(perm_d, total_d).reshape(RS, 16, 128).astype(bf16)
         last_start(finD_s, finD_r, 0, h)
-        rest.append(nn(perm_r, total))
-    t_second()
-    for h in range(2):
         total = widened(second_total(zE, rzE, 1, h), 80)
-        finE_s[h] = (nn(perm_e, total) + rest[h]).reshape(RS, 16, 128).astype(bf16)
+        finE_s[h] = (nn(perm_e, total) + nn(perm_r, total_d)).reshape(RS, 16, 128).astype(bf16)
         last_start(finE_s, finE_r, 1, h)
+        if h == 0:
+            t_last()
 
     lhalo.wait_recv()
     taps_in = []
@@ -665,24 +666,23 @@
         latent = term if latent is None else latent + term
     for f in range(2):
         lat_out[f, 0] = latent[32 * f : 32 * f + 32].astype(bf16)
-    t_last()
 
     last_wait(finD_r, 0)
     for cc in range(2):
         total = last_total(finD_r, cc)
         g_out[pl.ds(48 + 2 * cc, 9, stride=4), :] = total[0:9]
         g_out[pl.ds(49 + 2 * cc, 7, stride=4), :] = total[9:16]
+    t_finish()
     last_wait(finE_r, 1)
     for cc in range(2):
         total = last_total(finE_r, cc)
         g_out[pl.ds(cc, 9, stride=2), :] = total[0:9]
         g_out[pl.ds(77 + 2 * cc, 2, stride=4), :] = total[9:11]
-    t_finish()
     for h in halo + chalo + phalo + [lhalo]:
         h.wait_send()
     for send in (a1s, a2s, a3s.at[0], a3s.at[1], a4s):
         wait_for(send.at[pl.ds(0, FR - 1)], sent)
-    for ref in (rcD, rlD, ryD, rzD, rc2, ry2, rzE, rcT, rzT, rxT, finT_s.at[pl.ds(0, 7)]):
+    for ref in (rcD, rlD, ryD, rzD, rc2, ry2, rzE, rcT, rzT, finT_s.at[pl.ds(0, 31)]):
         wait_for(ref, sent)
     for fin_s in (finD_s, finE_s):
         for h in range(2):
@@ -712,7 +712,7 @@
         vb(2, 2, 64, C),
         vb(FR, 16, 128), vb(FR, 16, 128), vb(FR, 16, 128), vb(FR, 16, 128),
         vb(2, FR, 16, 128), vb(2, FR, 16, 128), vb(FR, 16, 128), vb(FR, 16, 128),
-        vf(2, C, 128), vb(4, 64, C), vb(2, 2, 32, C), vb(2, 2, 32, C), vf(C, 128),
+        vf(2, C, 128), vb(2, 2, 32, C), vb(2, 2, 32, C), vf(C, 128),
         vb(2, 64, 512), vb(2, 64, 512), vb(2, FR, 16, 128), vb(3, C, 512),
         vf(9 * C, 512), vf(3 * C, C), vf(C, 3 * C), vf(C, C), vf(9 * C, C),
     ]
@@ -722,13 +722,13 @@
         if rows == 144:
             scratch += [vb(2, 2, n // 2, 128), vb(2, 2, n, 128), vb(2, 4, 144, 128), vb(2, 3, 144, 128)]
             scratch += [vb(2, 8, 224, 128), vb(8, 224, 128), vb(8, 224, 128), vb(7, 224, 128)]
-            scratch += [vb(4, 64, 128), vb(3, 64, 128), vb(8, 16, 128), vb(8, 16, 128)]
+            scratch += [vb(32, 16, 128), vb(32, 16, 128)]
         else:
             scratch += [vb(2, 3, n, 128)]
     scratch += [vb(2, 4, 80, 128), vb(2, 3, 80, 128)]
     scratch += [vb(2, 8, 16, 128), vb(16, 16, 128), vb(2, 8, 16, 128), vb(16, 16, 128)]
     scratch += [
-        dma((7,)), dma, dma((6,)), dma((5,)), dma((16,)), dma((4,)), dma((4,)), dma((4,)), dma((2,)), dma((11,)),
+        dma((7,)), dma, dma((6,)), dma((5,)), dma((16,)), dma((4,)), dma((4,)), dma((4,)), dma((2,)), dma((10,)),
     ]
     anywhere = pl.BlockSpec(memory_space=pl.ANY)
     inside = pl.BlockSpec(memory_space=pltpu.VMEM)

time: 53.3 us -> 52.4 us (0.983)
  Pallas kernels: 52.6 us -> 51.6 us
    pallas_call x1, Pallas kernels: 51.9 us -> 51 us  [per_device(): pl.pallas_call(kernel, out_shape=(vb(2, 1, 32, 512), vf(88, 128)), in_spe...]
where the time goes in v1:
time: 52.4 us; the launch traced here: 52.3 us
  Pallas kernels  51.6 us (98%)
  between operations  0.64 us (1%)
    pallas_call x1, Pallas kernels, per_device(): pl.pallas_call(kernel, out_shape=(vb(2, 1, 32, 512), vf(88, 128)), in_spe...  51 us

profile of v1, /device:TPU:1, one launch (start us, length us, event | category | flops | bytes accessed | tf_op | source)
XLA Modules:
  0.0 52.3 jit_solution(13953998300606525805)
XLA Ops:
  0.6 51.0 %shard_map.118 = (bf16[2,1,32,512]{3,2,1,0:T(8,128)(2,1)S(1)}, f32[88,128]{1,0:T(8,128)S(1)}) custom-call(bf16[2,2,64,256]{3,2,1,0:T(8,128)(2,1)} %x_hbm.1, bf16[2304,256]{1,0:T(8,128)(2,1)} %wsp_hbm.1, bf16[768,256]{1,0:T(8,128)(2,1)} %wt_hbm.1, bf16[256,768]{1,0:T(8,128)(2,1)} %wq_hbm.1, bf16[256,256]{1,0:T(8,128)(2,1)} %wo_hbm.1, ...), custom_call_target="tpu_custom_call" | custom-call | flops 3000000000 | bytes 10000000 | tf_op jit(solution)/shard_map/pallas_call | solution.py:735
  51.6 0.7 %shard_map.119 = (bf16[2,1,32,512]{3,2,1,0:T(8,128)(2,1)}, f32[18,128]{1,0:T(8,128)}, f32[6,128]{1,0:T(8,128)}, f32[6,128]{1,0:T(8,128)}, f32[2,128]{1,0:T(2,128)}, /*index=5*/f32[36,128]{1,0:T(8,128)}) custom-call(bf16[2,1,32,512]{3,2,1,0:T(8,128)(2,1)S(1)} %get-tuple-element.14.lat, f32[88,128]{1,0:T(8,128)S(1)} %get-tuple-element.15.g), custom_call_target="tpu_custom_call" | custom-call | tf_op jit(solution)/shard_map/pallas_call | solution.py:748

commit v2 on v1

--- a/solution.py
+++ b/solution.py
@@ -141,18 +141,6 @@
         tell((fr, dest))
     for s in range(2, RS - 1):
         tell((fr, (r + s) & 7))
-    for s in range(ZS):
-        zs = (z + s) & 7
-        for cc in range(2):
-            source = (zs * 4 + x, 2 * ((z + zs) & 3) + (c ^ cc))
-            if s or cc:
-                tell(source)
-            else:
-                pl.when(jnp.logical_not(own[0] | own[1]))(lambda source=source: tell(source))
-    for s in range(1, XS):
-        for dr in range(1, RS):
-            tell((z * 4 + ((x + s) & 3), (r + dr) & 7))
-
     loads = []
     for i, (src, dst) in enumerate(
         ((cot_hbm, cotv), (x_hbm, xv), (wsp_hbm, wsp), (wd_hbm, wd), (wt_hbm, wt), (wq_hbm, wq), (wo_hbm, wo))
@@ -206,7 +194,7 @@
         other = jnp.concatenate([nn(first[128:], tap(2, b)), nn(first[:128], tap(0, b))], axis=0)
         parts.append(mid + other)
     pl.semaphore_wait(
-        barrier, (FR - 1) + (RS - 1) + 21 + 2 * RS - jnp.where(own[0], 1, 0) - jnp.where(own[1], 1, 0)
+        barrier, (FR - 1) + (RS - 1)
     )
     halo = [
         remote(x_hbm.at[:, 1], halo_x.at[0], sent, hr.at[0], (fr, down)),
@@ -560,6 +548,7 @@
     grad_tb32 = grad_tb.astype(f32)
 
 
+    first_start(cD, rcD, yD, rlD, 0, 144, (0,))
     turned_second = second.astype(f32).T.astype(bf16)
     gt[0:C, :] = nn(turned_second, frame_shift(grad_tb32, -2).astype(bf16))
     gt[C : 2 * C, :] = nn(turned_second, frame_shift(grad_tb32, -1).astype(bf16))
@@ -571,23 +560,30 @@
     grad_second = grad_second + frame_shift(nt(grad_tb, wtk[0]), -2)
     grad_sb = (grad_t + act_grad(sp, grad_second)).astype(bf16)
 
-    first_start(cD, rcD, yD, rlD, 0, 144, (0,))
     first_halves(cD, rcD, yD, ryD, 0, 144, (1,))
-    t_start()
-    first_halves(cD, rcD, yD, ryD, 0, 144, (0,))
-
-    for h in phalo:
-        h.wait_recv()
-    rows_in = (masked(hp[0], not_top), a3r[0], a3r[1], masked(hp[1], not_bottom))
-    for hh in range(4):
-        put(tmp, unpack(rows_in[hh].astype(f32)))
+    def turn_rows(hh, rows):
+        put(tmp, unpack(rows.astype(f32)))
         cells = [every_fourth(tmp, ww) for ww in range(4)]
         for b in range(3):
             pair = jnp.concatenate([cells[b], cells[b + 1]], axis=0)
             at_[b, :, 128 * hh : 128 * hh + 128] = pair.T.astype(bf16)
-    for a in range(3):
+
+    def space_taps(a):
         for b in range(3):
             gs_[(3 * a + b) * C : (3 * a + b + 1) * C, :] = nn(at_[b, :, 128 * a : 128 * a + 256], grad_sb)
+
+    turn_rows(1, a3r[0])
+    turn_rows(2, a3r[1])
+    space_taps(1)
+    t_start()
+    first_halves(cD, rcD, yD, ryD, 0, 144, (0,))
+
+    for h in phalo:
+        h.wait_recv()
+    turn_rows(0, masked(hp[0], not_top))
+    turn_rows(3, masked(hp[1], not_bottom))
+    for a in (0, 2):
+        space_taps(a)
     pack_rows(read_2, c2, 72)
     core_start(c2, rc2, 1)
 

time: 52.4 us -> 51.9 us (level)
  no operation moved by 1% of the time
where the time goes in v2:
time: 51.9 us; the launch traced here: 51.8 us
  Pallas kernels  51.2 us (99%)
  between operations  0.64 us (1%)
    pallas_call x1, Pallas kernels, per_device(): pl.pallas_call(kernel, out_shape=(vb(2, 1, 32, 512), vf(88, 128)), in_spe...  50.5 us

profile of v2, /device:TPU:1, one launch (start us, length us, event | category | flops | bytes accessed | tf_op | source)
XLA Modules:
  0.0 51.8 jit_solution(800628332549119731)
XLA Ops:
  0.6 50.5 %shard_map.118 = (bf16[2,1,32,512]{3,2,1,0:T(8,128)(2,1)S(1)}, f32[88,128]{1,0:T(8,128)S(1)}) custom-call(bf16[2,2,64,256]{3,2,1,0:T(8,128)(2,1)} %x_hbm.1, bf16[2304,256]{1,0:T(8,128)(2,1)} %wsp_hbm.1, bf16[768,256]{1,0:T(8,128)(2,1)} %wt_hbm.1, bf16[256,768]{1,0:T(8,128)(2,1)} %wq_hbm.1, bf16[256,256]{1,0:T(8,128)(2,1)} %wo_hbm.1, ...), custom_call_target="tpu_custom_call" | custom-call | flops 3000000000 | bytes 10000000 | tf_op jit(solution)/shard_map/pallas_call | solution.py:731
  51.2 0.7 %shard_map.119 = (bf16[2,1,32,512]{3,2,1,0:T(8,128)(2,1)}, f32[18,128]{1,0:T(8,128)}, f32[6,128]{1,0:T(8,128)}, f32[6,128]{1,0:T(8,128)}, f32[2,128]{1,0:T(2,128)}, /*index=5*/f32[36,128]{1,0:T(8,128)}) custom-call(bf16[2,1,32,512]{3,2,1,0:T(8,128)(2,1)S(1)} %get-tuple-element.14.lat, f32[88,128]{1,0:T(8,128)S(1)} %get-tuple-element.15.g), custom_call_target="tpu_custom_call" | custom-call | tf_op jit(solution)/shard_map/pallas_call | solution.py:744

commit v3 on v2

--- a/solution.py
+++ b/solution.py
@@ -126,21 +126,6 @@
 
     places = (y, x)
 
-    barrier = pltpu.get_barrier_semaphore()
-
-    def tell(dev):
-        pl.semaphore_signal(barrier, inc=1, device_id=dev, device_id_type=MESH)
-
-    def far_first(n):
-        t = n >> 2
-        dz = 4 + (1 - 2 * (t & 1)) * ((t + 1) >> 1)
-        return ((z + dz) & 7) * 4 + ((x + n + 1) & 3)
-
-    lax.fori_loop(0, FR - 1, lambda n, carry: (tell((far_first(n), r)), carry)[1], 0)
-    for dest in (up, down):
-        tell((fr, dest))
-    for s in range(2, RS - 1):
-        tell((fr, (r + s) & 7))
     loads = []
     for i, (src, dst) in enumerate(
         ((cot_hbm, cotv), (x_hbm, xv), (wsp_hbm, wsp), (wd_hbm, wd), (wt_hbm, wt), (wq_hbm, wq), (wo_hbm, wo))
@@ -149,6 +134,21 @@
         cp.start()
         loads.append(cp)
 
+    barrier = pltpu.get_barrier_semaphore()
+
+    def tell(dev):
+        pl.semaphore_signal(barrier, inc=1, device_id=dev, device_id_type=MESH)
+
+    def far_first(n):
+        t = n >> 2
+        dz = 4 + (1 - 2 * (t & 1)) * ((t + 1) >> 1)
+        return ((z + dz) & 7) * 4 + ((x + n + 1) & 3)
+
+    lax.fori_loop(0, FR - 1, lambda n, carry: (tell((far_first(n), r)), carry)[1], 0)
+    for dest in (up, down):
+        tell((fr, dest))
+    for s in range(2, RS - 1):
+        tell((fr, (r + s) & 7))
     def a2a_start(send, recv, i):
         def step(n, carry):
             k = far_first(n)
@@ -597,6 +597,15 @@
             zD[h, 2 * p] = total[:144]
             zD[h, 2 * p + 1] = total[144:]
         second_start(zD, rzD, 0, h)
+    gap = jnp.zeros((8, 128), f32)
+    for h in range(2):
+        direct_wait(rc2, ry2, 1, h)
+        for p in range(2):
+            total = first_total(c2, rc2, ry2, h, p, 72)
+            zE[h, 2 * p] = jnp.concatenate([total[:72], gap], axis=0).astype(bf16)
+            zE[h, 2 * p + 1] = jnp.concatenate([total[72:], gap], axis=0).astype(bf16)
+        second_start(zE, rzE, 1, h)
+
     a2a_wait(a4r, 3)
     put(tmp, unpack(a4r[...].astype(f32)))
     first_col = lax.broadcasted_iota(jnp.int32, (32, C), 0) == 0
@@ -616,15 +625,6 @@
         for wp in range(2):
             lrow_s[f, wp] = cells_of[f][1][wp]
     lhalo = remote(lrow_s, lrow_r, sent, hr.at[3], (fr, down))
-    gap = jnp.zeros((8, 128), f32)
-    for h in range(2):
-        direct_wait(rc2, ry2, 1, h)
-        for p in range(2):
-            total = first_total(c2, rc2, ry2, h, p, 72)
-            zE[h, 2 * p] = jnp.concatenate([total[:72], gap], axis=0).astype(bf16)
-            zE[h, 2 * p + 1] = jnp.concatenate([total[72:], gap], axis=0).astype(bf16)
-        second_start(zE, rzE, 1, h)
-
     it, jt = iota2(128, C)
     dt, ut = it >> 4, it & 15
     perm_d = one_at(jt == jnp.where(ut < 9, 0, 63) + dt * 9 + ut)

time: 51.9 us -> 52.1 us (level)
  no operation moved by 1% of the time
where the time goes in v3:
time: 52.1 us; the launch traced here: 52 us
  Pallas kernels  51.3 us (98%)
  between operations  0.64 us (1%)
    pallas_call x1, Pallas kernels, per_device(): pl.pallas_call(kernel, out_shape=(vb(2, 1, 32, 512), vf(88, 128)), in_spe...  50.7 us

profile of v3, /device:TPU:1, one launch (start us, length us, event | category | flops | bytes accessed | tf_op | source)
XLA Modules:
  0.0 52.0 jit_solution(3212745582156110208)
XLA Ops:
  0.6 50.7 %shard_map.118 = (bf16[2,1,32,512]{3,2,1,0:T(8,128)(2,1)S(1)}, f32[88,128]{1,0:T(8,128)S(1)}) custom-call(bf16[2,2,64,256]{3,2,1,0:T(8,128)(2,1)} %x_hbm.1, bf16[2304,256]{1,0:T(8,128)(2,1)} %wsp_hbm.1, bf16[768,256]{1,0:T(8,128)(2,1)} %wt_hbm.1, bf16[256,768]{1,0:T(8,128)(2,1)} %wq_hbm.1, bf16[256,256]{1,0:T(8,128)(2,1)} %wo_hbm.1, ...), custom_call_target="tpu_custom_call" | custom-call | flops 3000000000 | bytes 10000000 | tf_op jit(solution)/shard_map/pallas_call | solution.py:731
  51.3 0.7 %shard_map.119 = (bf16[2,1,32,512]{3,2,1,0:T(8,128)(2,1)}, f32[18,128]{1,0:T(8,128)}, f32[6,128]{1,0:T(8,128)}, f32[6,128]{1,0:T(8,128)}, f32[2,128]{1,0:T(2,128)}, /*index=5*/f32[36,128]{1,0:T(8,128)}) custom-call(bf16[2,1,32,512]{3,2,1,0:T(8,128)(2,1)S(1)} %get-tuple-element.14.lat, f32[88,128]{1,0:T(8,128)S(1)} %get-tuple-element.15.g), custom_call_target="tpu_custom_call" | custom-call | tf_op jit(solution)/shard_map/pallas_call | solution.py:744

commit v4 on v2

--- a/solution.py
+++ b/solution.py
@@ -575,8 +575,8 @@
     turn_rows(1, a3r[0])
     turn_rows(2, a3r[1])
     space_taps(1)
+    first_halves(cD, rcD, yD, ryD, 0, 144, (0,))
     t_start()
-    first_halves(cD, rcD, yD, ryD, 0, 144, (0,))
 
     for h in phalo:
         h.wait_recv()

time: 51.9 us -> 52 us (level)
  no operation moved by 1% of the time
where the time goes in v4:
time: 52 us; the launch traced here: 51.9 us
  Pallas kernels  51.3 us (99%)
  between operations  0.64 us (1%)
    pallas_call x1, Pallas kernels, per_device(): pl.pallas_call(kernel, out_shape=(vb(2, 1, 32, 512), vf(88, 128)), in_spe...  50.6 us

profile of v4, /device:TPU:1, one launch (start us, length us, event | category | flops | bytes accessed | tf_op | source)
XLA Modules:
  0.0 51.9 jit_solution(16934689047476401864)
XLA Ops:
  0.6 50.6 %shard_map.118 = (bf16[2,1,32,512]{3,2,1,0:T(8,128)(2,1)S(1)}, f32[88,128]{1,0:T(8,128)S(1)}) custom-call(bf16[2,2,64,256]{3,2,1,0:T(8,128)(2,1)} %x_hbm.1, bf16[2304,256]{1,0:T(8,128)(2,1)} %wsp_hbm.1, bf16[768,256]{1,0:T(8,128)(2,1)} %wt_hbm.1, bf16[256,768]{1,0:T(8,128)(2,1)} %wq_hbm.1, bf16[256,256]{1,0:T(8,128)(2,1)} %wo_hbm.1, ...), custom_call_target="tpu_custom_call" | custom-call | flops 3000000000 | bytes 10000000 | tf_op jit(solution)/shard_map/pallas_call | solution.py:731
  51.3 0.7 %shard_map.119 = (bf16[2,1,32,512]{3,2,1,0:T(8,128)(2,1)}, f32[18,128]{1,0:T(8,128)}, f32[6,128]{1,0:T(8,128)}, f32[6,128]{1,0:T(8,128)}, f32[2,128]{1,0:T(2,128)}, /*index=5*/f32[36,128]{1,0:T(8,128)}) custom-call(bf16[2,1,32,512]{3,2,1,0:T(8,128)(2,1)S(1)} %get-tuple-element.14.lat, f32[88,128]{1,0:T(8,128)S(1)} %get-tuple-element.15.g), custom_call_target="tpu_custom_call" | custom-call | tf_op jit(solution)/shard_map/pallas_call | solution.py:744
